TPU v7x, 768 devices: a whole 4x8x12 slice. The times are simulated.
768 devices in a mesh: wide: 96 (over z, y), narrow: 8 (over x, core).
Axes of the slice: x: 4, y: 8, z: 12, core: 2. Of those that a mesh axis runs over, the one named last changes fastest.
Arguments:
- crop_hidden: bfloat16 [12288, 2048], P('wide', 'narrow'), may hold values from -6 to 6
- bottleneck_weight: bfloat16 [2048, 384], P('narrow'), may hold values from -0.125 to 0.125
- prototypes: bfloat16 [384, 65536], P(None, 'narrow'), may hold values from -6 to 6
- teacher_scores: bfloat16 [12288, 65536], P('wide', 'narrow'), may hold values from -1 to 1
Outputs:
- grad_hidden: bfloat16 [12288, 2048], P('wide', 'narrow')
- grad_weight: float32 [384, 2048], P('wide', 'narrow')
All inputs are finite; a program needn't handle non-finite values.
Results may differ from a plain program's by a relative error of at most 0.0065.
Values may be sent and summed in bfloat16 or wider, within the bound.
A program may use at most 32 MiB of HBM per device.

v0:
```python
import jax
import jax.numpy as jnp
from jax import lax
from jax.sharding import PartitionSpec as P

PROTO = 65536
ITERS = 3


TEACHER_TEMP = 0.07
STUDENT_TEMP = 0.1


def normalize(bottleneck):
    inv_norm = lax.rsqrt(jnp.sum(bottleneck * bottleneck, 1) + 1e-06)
    return (inv_norm, bottleneck * inv_norm[:, None])


def descend(inv_norm, unit_rows, unit_grad):
    radial = jnp.sum(unit_rows * unit_grad, 1)
    return (inv_norm[:, None] * (unit_grad - unit_rows * radial[:, None])).astype(jnp.bfloat16)


def shards(crop_hidden, bottleneck_weight, prototypes, teacher_scores):
    row_count = crop_hidden.shape[0]
    crop_total = row_count * lax.axis_size("wide")
    raw = prototypes.astype(jnp.float32)
    columns = (raw * lax.rsqrt(jnp.sum(raw * raw, 0) + 1e-06)[None, :]).astype(jnp.bfloat16)
    bottleneck = lax.psum(
        jnp.dot(crop_hidden, bottleneck_weight, preferred_element_type=jnp.float32), "narrow"
    )
    inv_norm, unit_rows = normalize(bottleneck)
    unit_bf16 = unit_rows.astype(jnp.bfloat16)
    student_exp = jnp.exp(
        jnp.dot(unit_bf16, columns, preferred_element_type=jnp.float32) / STUDENT_TEMP
    )
    local_total = jnp.sum(student_exp, 1)
    teacher_exp = jnp.exp(teacher_scores.astype(jnp.float32) / TEACHER_TEMP)
    row_scale = jnp.ones((row_count,), jnp.float32)
    col_scale = jnp.ones((columns.shape[1],), jnp.float32)
    softmax_total = local_total
    for iteration in range(ITERS):
        column_mass = lax.psum(jnp.sum(teacher_exp * row_scale[:, None], 0), "wide")
        col_scale = 1.0 / (PROTO * column_mass)
        row_mass, softmax_total = lax.psum(
            (jnp.sum(teacher_exp * col_scale[None, :], 1), local_total), "narrow"
        )
        row_scale = 1.0 / (crop_total * row_mass)
    scaled_rows = row_scale * crop_total
    target = teacher_exp * scaled_rows[:, None] * col_scale[None, :]
    score_grad = (student_exp / softmax_total[:, None] - target).astype(jnp.bfloat16)
    partial_grad = lax.dot_general(
        score_grad, columns, (((1,), (1,)), ((), ())), preferred_element_type=jnp.float32
    )
    unit_grad = lax.psum(partial_grad, "narrow") / STUDENT_TEMP
    bottle_grad = descend(inv_norm, unit_rows, unit_grad)
    grad_hidden = lax.dot_general(
        bottle_grad, bottleneck_weight, (((1,), (1,)), ((), ())), preferred_element_type=jnp.float32
    ).astype(jnp.bfloat16)
    grad_weight = lax.psum_scatter(
        lax.dot_general(
            bottle_grad, crop_hidden, (((0,), (0,)), ((), ())), preferred_element_type=jnp.float32
        ),
        "wide",
        scatter_dimension=0,
        tiled=True,
    )
    return (grad_hidden, grad_weight)


def solution(mesh):
    placed = (P("wide", "narrow"), P("narrow", None), P(None, "narrow"), P("wide", "narrow"))
    return jax.shard_map(
        shards,
        mesh=mesh,
        in_specs=placed,
        out_specs=(P("wide", "narrow"), P("wide", "narrow")),
        check_vma=False,
    )
```

profile of v0, /device:TPU:1, one launch (start us, length us, event | category | flops | bytes accessed | tf_op | source)
XLA Modules:
  0.0 1612.4 jit_solution(9166472536305190683)
XLA Ops:
  7.2 0.0 copy-start
  7.2 0.0 copy-start.1
  7.2 0.0 all-reduce.6.cloned.1.call-start
  7.2 0.9 copy-done
  8.1 1.7 fusion.14
  9.8 0.0 all-reduce.6.cloned.1.call-update
  9.8 0.0 all-reduce.8.cloned.1.call-start
  9.9 4.1 fusion
  14.0 0.0 copy-done.1
  14.0 0.7 fusion.6
  14.8 344.2 %psum.65 = f32[8192]{0:T(1024)S(1)} all-reduce(f32[8192]{0:T(1024)S(1)} %fusion.6), channel_id=1, replica_groups=mesh['wide'=96,'narrow'=8] {'wide'}, use_global_device_ids=true, to_apply=%region_6.0 | all-reduce | flops 8192 | bytes 65536 | tf_op jit(solution)/shard_map/psum | solution.py:43
  359.0 0.9 multiply_reduce_fusion.4
  359.9 94.9 %psum.66 = f32[128]{0:T(128)S(1)} all-reduce(f32[128]{0:T(128)S(1)} %multiply_reduce_fusion.4), channel_id=1, replica_groups=mesh['wide'=96,'narrow'=8] {'narrow'}, use_global_device_ids=true, to_apply=%region_8.0 | all-reduce | flops 128 | bytes 1024 | tf_op jit(solution)/shard_map/psum | solution.py:45
  454.8 0.9 multiply_reduce_fusion.3
  455.7 328.2 %psum.67 = f32[8192]{0:T(1024)S(1)} all-reduce(f32[8192]{0:T(1024)S(1)} %multiply_reduce_fusion.3), channel_id=1, replica_groups=mesh['wide'=96,'narrow'=8] {'wide'}, use_global_device_ids=true, to_apply=%region_10.0 | all-reduce | flops 8192 | bytes 65536 | tf_op jit(solution)/shard_map/psum | solution.py:43
  783.8 0.9 multiply_reduce_fusion.2
  784.7 94.5 %psum.68 = f32[128]{0:T(128)S(1)} all-reduce(f32[128]{0:T(128)S(1)} %multiply_reduce_fusion.2), channel_id=1, replica_groups=mesh['wide'=96,'narrow'=8] {'narrow'}, use_global_device_ids=true, to_apply=%region_12.0 | all-reduce | flops 128 | bytes 1024 | tf_op jit(solution)/shard_map/psum | solution.py:45
  879.3 0.9 multiply_reduce_fusion.1
  880.2 328.2 %psum.69 = f32[8192]{0:T(1024)S(1)} all-reduce(f32[8192]{0:T(1024)S(1)} %multiply_reduce_fusion.1), channel_id=1, replica_groups=mesh['wide'=96,'narrow'=8] {'wide'}, use_global_device_ids=true, to_apply=%region_14.0 | all-reduce | flops 8192 | bytes 65536 | tf_op jit(solution)/shard_map/psum | solution.py:43
  1208.3 0.9 multiply_reduce_fusion
  1209.3 0.0 all-reduce.6.cloned.1.call-done
  1209.3 1.0 multiply_reduce_fusion.6
  1210.3 6.9 fusion.13
  1217.2 94.7 %all-reduce.1 = (f32[128]{0:T(128)S(1)}, f32[128]{0:T(128)S(1)}) all-reduce(f32[128]{0:T(128)S(1)} %multiply_reduce_fusion, f32[128]{0:T(128)S(1)} %get-tuple-element.4), channel_id=1, replica_groups=mesh['wide'=96,'narrow'=8] {'narrow'}, use_global_device_ids=true, to_apply=%region_16.0 | all-reduce | flops 256 | bytes 2048 | tf_op jit(solution)/shard_map/psum | solution.py:45
  1311.9 0.0 copy-start.2
  1311.9 0.0 copy-start.3
  1311.9 7.2 fusion.3
  1319.1 0.0 all-reduce.8.cloned.1.call-update
  1319.1 0.0 all-reduce.10.cloned.1.call-start
  1319.1 62.2 %all-reduce.8.cloned.1.call-done = f32[128,384]{1,0:T(8,128)} async-done(((f32[128,384]{1,0:T(8,128)}), f32[128,384]{1,0:T(8,128)}) %all-reduce.8.cloned.1.call-update) | async-done | bytes 196624 | tf_op jit(solution)/shard_map/psum | solution.py:55
  1381.3 0.0 copy-done.2
  1381.3 1.1 multiply_reduce_fusion.5
  1382.4 1.0 multiply_convert_fusion
  1383.5 0.0 copy-done.3
  1383.5 1.0 fusion.15
  1384.5 0.0 all-reduce.10.cloned.1.call-update
  1384.5 1.3 dynamic-slice
  1386.4 0.8 convolution_convert_fusion
  1387.3 217.3 %all-reduce.10.cloned.1.call-done = f32[384,256]{1,0:T(8,128)} async-done(((f32[384,256]{1,0:T(8,128)}), f32[384,256]{1,0:T(8,128)}) %all-reduce.10.cloned.1.call-update) | async-done | bytes 393232
  1604.6 1.3 constant_dynamic-slice_fusion
  (8 shorter events, 0.1 us)
Async XLA Ops:
  7.2 0.9 copy-start
  7.2 6.8 copy-start.1
  7.2 1202.1 %all-reduce.6.cloned.1.call-start = ((), (), s32[]{:S(2)}) async-start(), calls=%async_computation | async-start | bytes 393216 | tf_op jit(solution)/shard_map/psum | solution.py:29
  9.8 1371.5 %all-reduce.8.cloned.1.call-start = ((), (), s32[]{:S(2)}) async-start(), calls=%async_computation.1 | async-start | bytes 393216 | tf_op jit(solution)/shard_map/psum | solution.py:55
  1311.9 69.4 %copy-start.2 = (f32[128,384]{1,0:T(8,128)S(1)}, f32[128,384]{1,0:T(8,128)}, u32[]{:S(2)}) copy-start(f32[128,384]{1,0:T(8,128)} %all-reduce.6.cloned.1.call-done) | copy-start | bytes 589828
  1311.9 71.6 %copy-start.3 = (bf16[128,256]{1,0:T(8,128)(2,1)S(1)}, bf16[128,256]{1,0:T(8,128)(2,1)}, u32[]{:S(2)}) copy-start(bf16[128,256]{1,0:T(8,128)(2,1)} %param.4) | copy-start | bytes 196612
  1319.1 285.5 %all-reduce.10.cloned.1.call-start = ((), (), s32[]{:S(2)}) async-start(), calls=%async_computation.2 | async-start | bytes 786432
Sparse Core Ops, SparseCore 0:
  10.3 83.0 all-reduce.5
  1319.2 62.0 all-reduce.7
  1385.0 219.5 all-reduce.9
where the time goes:
time: 1620 us; the launch traced here: 1610 us
  blocking collectives  1280 us (79%)
  waiting for transfers between devices  280 us (17%)
  matrix products  17.6 us (1%)
    psum x3, blocking collectives, shards(): column_mass = lax.psum(jnp.sum(teacher_exp * row_scale[:, None], 0), 'wide')  1000 us
    psum x3, blocking collectives, shards(): lax.psum((jnp.sum(teacher_exp * col_scale[None, :], 1), local_total), 'na...  284 us
    unnamed x4, waiting for transfers between devices  217 us
    psum x1, waiting for transfers between devices, shards(): unit_grad = lax.psum(partial_grad, 'narrow') / STUDENT_TEMP  62.2 us
  transfers between devices with their start and end apart: 3, of which 2 were waited for; matrix products, arithmetic and copies ran while one was open for 1% of the time, Pallas kernels for 0%

commit v1 on v0

v1 whole, which is shorter than its diff:
```python
import jax
import jax.numpy as jnp
from jax import lax
from jax.experimental import pallas as pl
from jax.experimental.pallas import tpu as pltpu
from jax.sharding import PartitionSpec as P

PROTO = 65536
CROPS = 12288
BOT = 384
ITERS = 3
TEACHER_TEMP = 0.07
STUDENT_TEMP = 0.1

Z, Y, N = 12, 8, 8
ROWS = CROPS // (Z * Y)
OWN = ROWS // N
COLS = PROTO // N
LANES = 128
PIECE = COLS // Y
SUB = PIECE // LANES
HIDB = 2048 // N
WIDE = BOT + LANES
GROUP = BOT // Y

F32 = jnp.float32
BF16 = jnp.bfloat16
MESH = pl.DeviceIdType.MESH

FAR8 = (4, 3, 5, 2, 6, 1, 7)
NEAR8 = (1, 7, 2, 6, 3, 5, 4)
FAR12 = (6, 5, 7, 4, 8, 3, 9, 2, 10, 1, 11)
NT = (((1,), (1,)), ((), ()))


def kernel(
    x_hbm, w_hbm, p_hbm, t_hbm, gh_ref, gw_ref,
    tin, raw, wv, xall, texp, inv_col, cbuf, yrecv, zsrc, zrecv, vall,
    nsrc, nrecv, ub, bpart, brecv, ball, unit_own, inv_own, sbuf, gbuf,
    egm, egr, eg_own, tgm, tgr, bgall, perm, bts, btr, gwf, gwz, gwr,
    load_sem, proto_sem, send_sem, recv_sem, v_sem, bt_sem,
):
    w = lax.axis_index("wide")
    n = lax.axis_index("narrow")
    z = lax.div(w, Y)
    y = lax.rem(w, Y)

    def dev_y(d):
        return (z * Y + lax.rem(y + d, Y), n)

    def dev_z(d):
        return (lax.rem(z + d, Z) * Y + y, n)

    def dev_n(d):
        return (w, lax.rem(n + d, N))

    barrier = pltpu.get_barrier_semaphore()
    for d in FAR12:
        pl.semaphore_signal(barrier, inc=1, device_id=dev_z(d), device_id_type=MESH)
    for d in FAR8:
        pl.semaphore_signal(barrier, inc=1, device_id=dev_y(d), device_id_type=MESH)
    for d in FAR8:
        pl.semaphore_signal(barrier, inc=1, device_id=dev_n(d), device_id_type=MESH)

    order = [lax.rem(y + d, Y) for d in FAR8] + [y]
    load_x = pltpu.make_async_copy(x_hbm, xall.at[y], load_sem.at[0])
    load_w = pltpu.make_async_copy(w_hbm, wv, load_sem.at[1])
    load_x.start()
    load_w.start()

    def columns(p):
        return pl.ds(pl.multiple_of(p * PIECE, PIECE), PIECE)

    load_t = []
    for k, p in enumerate(order):
        load_t.append(
            pltpu.make_async_copy(t_hbm.at[:, columns(p)], tin.at[p], load_sem.at[2 + k])
        )
        load_t[-1].start()
    load_p = []
    for p in range(Y):
        load_p.append(
            pltpu.make_async_copy(p_hbm.at[:, columns(p)], raw.at[p], proto_sem.at[p])
        )
        load_p[-1].start()

    sends = []

    def send(src, dst, phase, sem, device):
        pltpu.make_async_remote_copy(
            src, dst, send_sem.at[phase], sem, device_id=device, device_id_type=MESH
        ).start()

    def wait_all(ref, sem):
        pltpu.make_async_copy(ref, ref, sem).wait()

    PH_B, PH_U, PH_X, PH_EG, PH_TG, PH_BG, PH_BT, PH_GW, PH_IT = range(9)

    load_x.wait()
    load_w.wait()
    bpart[...] = jnp.dot(xall[y], wv[...], preferred_element_type=F32).reshape(N, OWN, BOT)

    def first_piece(k, p):
        load_t[k].wait()
        for s in range(SUB):
            e = jnp.exp(tin[p, :, s * LANES : (s + 1) * LANES].astype(F32) * (1.0 / TEACHER_TEMP))
            texp[p * SUB + s] = e
            cbuf[0, p, s : s + 1, :] = jnp.sum(e, 0, keepdims=True)

    def mass_piece(it, p, rows):
        for s in range(SUB):
            cbuf[it, p, s : s + 1, :] = jnp.sum(texp[p * SUB + s] * rows, 0, keepdims=True)

    def send_columns(it, k):
        d = FAR8[k]
        send(
            cbuf.at[it, order[k]], yrecv.at[it, d - 1],
            PH_IT + 4 * it, recv_sem.at[PH_IT + 4 * it], dev_y(d),
        )

    def norm_piece(p):
        load_p[p].wait()
        for s in range(SUB):
            c = raw[p, :, s * LANES : (s + 1) * LANES].astype(F32)
            inv_col[p, s : s + 1, :] = lax.rsqrt(jnp.sum(c * c, 0, keepdims=True) + 1e-06)

    def own_rows():
        wait_all(brecv, recv_sem.at[PH_B])
        b = bpart[n]
        for d in range(N - 1):
            b = b + brecv[d]
        inv = lax.rsqrt(jnp.sum(b * b, 1, keepdims=True) + 1e-06)
        unit = b * inv
        unit_own[...] = unit
        inv_own[...] = jnp.broadcast_to(inv, (OWN, LANES))
        ball[n] = unit.astype(BF16)
        for d in FAR8:
            send(ball.at[n], ball.at[n], PH_U, recv_sem.at[PH_U], dev_n(d))

    def all_rows():
        wait_all(ball.at[pl.ds(0, N - 1)], recv_sem.at[PH_U])

    def student_piece(p):
        sbuf[...] = jnp.dot(
            ball[...].reshape(ROWS, BOT), raw[p], preferred_element_type=F32
        )
        total = jnp.zeros((ROWS, LANES), F32)
        for s in range(SUB):
            at = slice(s * LANES, (s + 1) * LANES)
            inv = inv_col[p, s : s + 1, :]
            e = jnp.exp(sbuf[:, at] * (inv * (1.0 / STUDENT_TEMP)))
            total = total + e
            gbuf[:, at] = (e * inv).astype(BF16)
        part = lax.dot_general(gbuf[...], raw[p], NT, preferred_element_type=F32)
        part = part.reshape(N, OWN, BOT)
        total = total.reshape(N, OWN, LANES)
        if p == 0:
            egm[:, :, :BOT] = part
            egm[:, :, BOT:] = total
        else:
            egm[:, :, :BOT] += part
            egm[:, :, BOT:] += total

    def send_student():
        for d in FAR8:
            send(egm.at[lax.rem(n + d, N)], egr.at[d - 1], PH_EG, recv_sem.at[PH_EG], dev_n(d))

    def own_student():
        wait_all(egr, recv_sem.at[PH_EG])
        e = egm[n]
        for d in range(N - 1):
            e = e + egr[d]
        total = jnp.sum(e[:, BOT:], 1, keepdims=True)
        eg_own[...] = e[:, :BOT] / total

    def permutation():
        k = lax.broadcasted_iota(jnp.int32, (BOT, BOT), 0)
        c = lax.broadcasted_iota(jnp.int32, (BOT, BOT), 1)
        per = GROUP // Z
        ky = lax.div(k, GROUP)
        kz = lax.div(lax.rem(k, GROUP), per)
        kb = lax.rem(k, per)
        perm[...] = jnp.where(c == kz * (per * Y) + ky * per + kb, 1.0, 0.0).astype(BF16)

    def share_hidden(*ds):
        for d in ds:
            send(xall.at[y], xall.at[y], PH_X, recv_sem.at[PH_X], dev_y(d))

    work = {
        (0, "y"): [lambda p=p: norm_piece(p) for p in range(Y)],
        (0, "z"): [lambda: share_hidden(1, 7, 2, 6), own_rows],
        (0, "v"): [all_rows, lambda: student_piece(0), lambda: student_piece(1)],
        (0, "n"): [lambda: student_piece(2), lambda: student_piece(3)],
        (1, "y"): [lambda: student_piece(4), lambda: student_piece(5)],
        (1, "z"): [
            lambda: share_hidden(3, 5),
            lambda: student_piece(6), lambda: student_piece(7), send_student,
        ],
        (1, "v"): [],
        (1, "n"): [permutation],
        (2, "y"): [own_student],
        (2, "z"): [lambda: share_hidden(4)],
        (2, "v"): [],
    }

    def beside(it, name):
        for item in work[(it, name)]:
            item()

    for it in range(ITERS):
        ph = PH_IT + 4 * it
        if it == 0:
            for k in range(Y):
                first_piece(k, order[k])
            pl.semaphore_wait(barrier, (Z - 1) + (Y - 1) + (N - 1))
            for k in range(Y - 1):
                send_columns(0, k)
            for d in FAR8:
                send(bpart.at[lax.rem(n + d, N)], brecv.at[d - 1], PH_B, recv_sem.at[PH_B], dev_n(d))
        else:
            rows = ub[...]
            for k in range(Y):
                mass_piece(it, order[k], rows)
                if k < Y - 1:
                    send_columns(it, k)
        beside(it, "y")
        wait_all(yrecv.at[it], recv_sem.at[ph])
        mass = cbuf[it, y]
        for d in range(Y - 1):
            mass = mass + yrecv[it, d]
        zsrc[it] = mass
        for d in FAR12:
            send(zsrc.at[it], zrecv.at[it, d - 1], ph + 1, recv_sem.at[ph + 1], dev_z(d))
        beside(it, "z")
        wait_all(zrecv.at[it], recv_sem.at[ph + 1])
        for d in range(Z - 1):
            mass = mass + zrecv[it, d]
        vall[it, y] = 1.0 / (PROTO * mass)
        for d in FAR8:
            send(vall.at[it, y], vall.at[it, y], ph + 2, v_sem.at[it, d - 1], dev_y(d))
        beside(it, "v")

        acc = jnp.zeros((ROWS, LANES), F32)
        for k, d in enumerate((0,) + NEAR8):
            p = lax.rem(y - d + Y, Y)
            if d:
                wait_all(vall.at[it, p], v_sem.at[it, d - 1])
            if it < ITERS - 1:
                for s in range(SUB):
                    acc = acc + texp[p * SUB + s] * vall[it, p, s : s + 1, :]
            else:
                for s in range(SUB):
                    tv = texp[p * SUB + s] * vall[it, p, s : s + 1, :]
                    acc = acc + tv
                    gbuf[:, s * LANES : (s + 1) * LANES] = (tv * inv_col[p, s : s + 1, :]).astype(BF16)
                part = lax.dot_general(gbuf[...], raw[p], NT, preferred_element_type=F32)
                part = part.reshape(N, OWN, BOT)
                if k == 0:
                    tgm[:, :, :BOT] = part
                else:
                    tgm[:, :, :BOT] += part
        if it < ITERS - 1:
            nsrc[it] = jnp.sum(acc.T, 0, keepdims=True)
            for d in FAR8:
                send(nsrc.at[it], nrecv.at[it, d - 1], ph + 3, recv_sem.at[ph + 3], dev_n(d))
            beside(it, "n")
            wait_all(nrecv.at[it], recv_sem.at[ph + 3])
            total = nsrc[it]
            for d in range(N - 1):
                total = total + nrecv[it, d]
            scale = 1.0 / (CROPS * total)
            ub[...] = jnp.broadcast_to(scale, (LANES, ROWS)).T
        else:
            tgm[:, :, BOT:] = acc.reshape(N, OWN, LANES)

    for d in FAR8:
        send(tgm.at[lax.rem(n + d, N)], tgr.at[d - 1], PH_TG, recv_sem.at[PH_TG], dev_n(d))
    wait_all(tgr, recv_sem.at[PH_TG])
    t = tgm[n]
    for d in range(N - 1):
        t = t + tgr[d]
    scale = 1.0 / (CROPS * jnp.sum(t[:, BOT:], 1, keepdims=True))
    unit = unit_own[...]
    ug = (eg_own[...] - t[:, :BOT] * (scale * CROPS)) * (1.0 / STUDENT_TEMP)
    radial = jnp.sum(unit * ug, 1, keepdims=True)
    bgall[n] = (inv_own[:, :1] * (ug - unit * radial)).astype(BF16)
    for d in FAR8:
        send(bgall.at[n], bgall.at[n], PH_BG, recv_sem.at[PH_BG], dev_n(d))
    wait_all(bgall.at[pl.ds(0, N - 1)], recv_sem.at[PH_BG])

    bg = bgall[...].reshape(ROWS, BOT)
    bts[...] = (
        lax.dot_general(perm[...], bg, NT, preferred_element_type=F32)
        .astype(BF16)
        .reshape(Y, GROUP, ROWS)
    )
    for d in FAR8:
        send(bts.at[lax.rem(y + d, Y)], btr.at[d - 1], PH_BT, bt_sem.at[d - 1], dev_y(d))
    gh_ref[...] = lax.dot_general(bg, wv[...], NT, preferred_element_type=F32).astype(BF16)
    wait_all(xall.at[pl.ds(0, Y - 1)], recv_sem.at[PH_X])
    gw = jnp.dot(bts[y], xall[y], preferred_element_type=F32)
    for d in NEAR8:
        wait_all(btr.at[d - 1], bt_sem.at[d - 1])
        gw = gw + jnp.dot(btr[d - 1], xall[lax.rem(y - d + Y, Y)], preferred_element_type=F32)
    gwf[...] = gw
    for i in range(Z):
        gwz[i, 0:4, :] = gwf[4 * i : 4 * i + 4, :LANES]
        gwz[i, 4:8, :] = gwf[4 * i : 4 * i + 4, LANES:]
    for d in FAR12:
        send(gwz.at[lax.rem(z + d, Z)], gwr.at[d - 1], PH_GW, recv_sem.at[PH_GW], dev_z(d))
    wait_all(brecv, send_sem.at[PH_B])
    wait_all(ball.at[pl.ds(0, N - 1)], send_sem.at[PH_U])
    wait_all(xall.at[pl.ds(0, Y - 1)], send_sem.at[PH_X])
    wait_all(egr, send_sem.at[PH_EG])
    wait_all(tgr, send_sem.at[PH_TG])
    wait_all(bgall.at[pl.ds(0, N - 1)], send_sem.at[PH_BG])
    wait_all(btr, send_sem.at[PH_BT])
    for it in range(ITERS):
        ph = PH_IT + 4 * it
        wait_all(yrecv.at[it], send_sem.at[ph])
        wait_all(zrecv.at[it], send_sem.at[ph + 1])
        wait_all(vall.at[it, pl.ds(0, Y - 1)], send_sem.at[ph + 2])
        if it < ITERS - 1:
            wait_all(nrecv.at[it], send_sem.at[ph + 3])
    wait_all(gwr, send_sem.at[PH_GW])
    wait_all(gwr, recv_sem.at[PH_GW])
    out = gwz[z]
    for d in range(Z - 1):
        out = out + gwr[d]
    gw_ref[...] = out


def shards(crop_hidden, bottleneck_weight, prototypes, teacher_scores):
    phases = 8 + 4 * ITERS
    vmem = pltpu.VMEM
    gh, gw = pl.pallas_call(
        kernel,
        out_shape=(
            jax.ShapeDtypeStruct((ROWS, HIDB), BF16),
            jax.ShapeDtypeStruct((8, LANES), F32),
        ),
        in_specs=[pl.BlockSpec(memory_space=pl.ANY)] * 4,
        out_specs=(pl.BlockSpec(memory_space=vmem), pl.BlockSpec(memory_space=vmem)),
        scratch_shapes=[
            vmem((Y, ROWS, PIECE), BF16),
            vmem((Y, BOT, PIECE), BF16),
            vmem((HIDB, BOT), BF16),
            vmem((Y, ROWS, HIDB), BF16),
            vmem((Y * SUB, ROWS, LANES), F32),
            vmem((Y, SUB, LANES), F32),
            vmem((ITERS, Y, SUB, LANES), F32),
            vmem((ITERS, Y - 1, SUB, LANES), F32),
            vmem((ITERS, SUB, LANES), F32),
            vmem((ITERS, Z - 1, SUB, LANES), F32),
            vmem((ITERS, Y, SUB, LANES), F32),
            vmem((ITERS - 1, 1, ROWS), F32),
            vmem((ITERS - 1, N - 1, 1, ROWS), F32),
            vmem((ROWS, LANES), F32),
            vmem((N, OWN, BOT), F32),
            vmem((N - 1, OWN, BOT), F32),
            vmem((N, OWN, BOT), BF16),
            vmem((OWN, BOT), F32),
            vmem((OWN, LANES), F32),
            vmem((ROWS, PIECE), F32),
            vmem((ROWS, PIECE), BF16),
            vmem((N, OWN, WIDE), F32),
            vmem((N - 1, OWN, WIDE), F32),
            vmem((OWN, BOT), F32),
            vmem((N, OWN, WIDE), F32),
            vmem((N - 1, OWN, WIDE), F32),
            vmem((N, OWN, BOT), BF16),
            vmem((BOT, BOT), BF16),
            vmem((Y, GROUP, ROWS), BF16),
            vmem((Y - 1, GROUP, ROWS), BF16),
            vmem((GROUP, HIDB), F32),
            vmem((Z, 8, LANES), F32),
            vmem((Z - 1, 8, LANES), F32),
            pltpu.SemaphoreType.DMA((2 + Y,)),
            pltpu.SemaphoreType.DMA((Y,)),
            pltpu.SemaphoreType.DMA((phases,)),
            pltpu.SemaphoreType.DMA((phases,)),
            pltpu.SemaphoreType.DMA((ITERS, Y - 1)),
            pltpu.SemaphoreType.DMA((Y - 1,)),
        ],
        compiler_params=pltpu.CompilerParams(
            collective_id=0, has_side_effects=True, vmem_limit_bytes=60 * 1024 * 1024
        ),
        name="sinkhorn_head",
    )(crop_hidden, bottleneck_weight, prototypes, teacher_scores)
    half = HIDB // 2
    return gh, jnp.concatenate([gw[:4, :half], gw[4:, :half]], axis=1)


def solution(mesh):
    placed = (P("wide", "narrow"), P("narrow", None), P(None, "narrow"), P("wide", "narrow"))
    return jax.shard_map(
        shards,
        mesh=mesh,
        in_specs=placed,
        out_specs=(P("wide", "narrow"), P("wide", "narrow")),
        check_vma=False,
    )
```

time: 1620 us -> 95.2 us (0.06)
  blocking collectives: 1280 us -> 0 us
  waiting for transfers between devices: 280 us -> 0 us
  Pallas kernels: 0 us -> 91.5 us
  matrix products: 17.6 us -> 0 us
    psum x6 -> x0, blocking collectives: 1280 us -> none  [the longest x3 1000 us: shards(): column_mass = lax.psum(jnp.sum(teacher_exp * row_scale[:, None], 0), 'wide')]
    unnamed x4 -> x0, waiting for transfers between devices: 217 us -> none
    pallas_call x0 -> x1, Pallas kernels: none -> 91.5 us  [shards(): pl.pallas_call(kernel, out_shape=(jax.ShapeDtypeStruct((ROWS, HIDB), BF16...]
    psum x2 -> x0, waiting for transfers between devices: 62.2 us -> none  [the longest x1 62.2 us: shards(): unit_grad = lax.psum(partial_grad, 'narrow') / STUDENT_TEMP]
    dot_general x5 -> x0, matrix products: 17.6 us -> none  [the longest x1 7.16 us: shards(): lax.dot_general(score_grad, columns, (((1,), (1,)), ((), ())), preferred_...]
  transfers between devices with their start and end apart: 3 -> 0, of which waited for: 2 -> 0; matrix products, arithmetic and copies ran while one was open for 1% -> 0% of each run, Pallas kernels for 0% -> 0%
where the time goes in v1:
time: 95.2 us; the launch traced here: 95 us
  Pallas kernels  91.5 us (96%)
  local copies, waits for them, and re-layouts  2.24 us (2%)
    pallas_call x1, Pallas kernels, shards(): pl.pallas_call(kernel, out_shape=(jax.ShapeDtypeStruct((ROWS, HIDB), BF16...  91.5 us

profile of v1, /device:TPU:1, one launch (start us, length us, event | category | flops | bytes accessed | tf_op | source)
XLA Modules:
  0.0 95.0 jit_solution(7781404203455768725)
XLA Ops:
  0.6 91.5 %sinkhorn_head.1 = (bf16[128,256]{1,0:T(8,128)(2,1)}, f32[8,128]{1,0:T(8,128)}) custom-call(bf16[128,256]{1,0:T(8,128)(2,1)} %x_hbm.1, bf16[256,384]{1,0:T(8,128)(2,1)} %w_hbm.1, bf16[384,8192]{1,0:T(8,128)(2,1)} %p_hbm.1, bf16[128,8192]{1,0:T(8,128)(2,1)} %t_hbm.1), custom_call_target="tpu_custom_call" | custom-call | tf_op jit(solution)/shard_map/sinkhorn_head/pallas_call | solution.py:336
  92.1 0.8 fusion
  92.9 0.6 pad_maximum_fusion
  93.5 1.5 %copy.7 = bf16[128,256]{1,0:T(8,128)(2,1)} copy(bf16[128,256]{1,0:T(8,128)(2,1)} %get-tuple-element.10) | data formatting | bytes 131072

commit v2 on v1

--- a/solution.py
+++ b/solution.py
@@ -21,6 +21,8 @@
 SUB = PIECE // LANES
 HIDB = 2048 // N
 WIDE = BOT + LANES
+GROUPS = ROWS // 8
+TOTALS = 1
 GROUP = BOT // Y
 
 F32 = jnp.float32
@@ -36,8 +38,8 @@
 def kernel(
     x_hbm, w_hbm, p_hbm, t_hbm, gh_ref, gw_ref,
     tin, raw, wv, xall, texp, inv_col, cbuf, yrecv, zsrc, zrecv, vall,
-    nsrc, nrecv, ub, bpart, brecv, ball, unit_own, inv_own, sbuf, gbuf,
-    egm, egr, eg_own, tgm, tgr, bgall, perm, bts, btr, gwf, gwz, gwr,
+    nsrc, nrecv, ub, kappa, bpart, brecv, ball, unit_own, inv_own, sbuf, gbuf,
+    egm, egr, eg_own, eg_less, tgf, tgm, tgr, bgall, perm, bts, btr, gwf, gwz, gwr,
     load_sem, proto_sem, send_sem, recv_sem, v_sem, bt_sem,
 ):
     w = lax.axis_index("wide")
@@ -65,8 +67,6 @@
     order = [lax.rem(y + d, Y) for d in FAR8] + [y]
     load_x = pltpu.make_async_copy(x_hbm, xall.at[y], load_sem.at[0])
     load_w = pltpu.make_async_copy(w_hbm, wv, load_sem.at[1])
-    load_x.start()
-    load_w.start()
 
     def columns(p):
         return pl.ds(pl.multiple_of(p * PIECE, PIECE), PIECE)
@@ -77,6 +77,8 @@
             pltpu.make_async_copy(t_hbm.at[:, columns(p)], tin.at[p], load_sem.at[2 + k])
         )
         load_t[-1].start()
+    load_x.start()
+    load_w.start()
     load_p = []
     for p in range(Y):
         load_p.append(
@@ -95,10 +97,6 @@
         pltpu.make_async_copy(ref, ref, sem).wait()
 
     PH_B, PH_U, PH_X, PH_EG, PH_TG, PH_BG, PH_BT, PH_GW, PH_IT = range(9)
-
-    load_x.wait()
-    load_w.wait()
-    bpart[...] = jnp.dot(xall[y], wv[...], preferred_element_type=F32).reshape(N, OWN, BOT)
 
     def first_piece(k, p):
         load_t[k].wait()
@@ -172,6 +170,7 @@
             e = e + egr[d]
         total = jnp.sum(e[:, BOT:], 1, keepdims=True)
         eg_own[...] = e[:, :BOT] / total
+        eg_less[...] = e[:, :BOT] * kappa[pl.ds(pl.multiple_of(n * OWN, OWN), OWN), :1]
 
     def permutation():
         k = lax.broadcasted_iota(jnp.int32, (BOT, BOT), 0)
@@ -181,6 +180,14 @@
         kz = lax.div(lax.rem(k, GROUP), per)
         kb = lax.rem(k, per)
         perm[...] = jnp.where(c == kz * (per * Y) + ky * per + kb, 1.0, 0.0).astype(BF16)
+
+    def row_tile(a, first):
+        lane = lax.broadcasted_iota(jnp.int32, (8, LANES), 1)
+        tile = jnp.zeros((8, LANES), F32)
+        for g in range(GROUPS):
+            mass = jnp.sum(a[8 * g : 8 * g + 8], 1, keepdims=True)
+            tile = jnp.where(lane == first + g, mass, tile)
+        return tile
 
     def share_hidden(*ds):
         for d in ds:
@@ -210,11 +217,19 @@
     for it in range(ITERS):
         ph = PH_IT + 4 * it
         if it == 0:
-            for k in range(Y):
+            for k in range(4):
                 first_piece(k, order[k])
             pl.semaphore_wait(barrier, (Z - 1) + (Y - 1) + (N - 1))
-            for k in range(Y - 1):
+            for k in range(4):
                 send_columns(0, k)
+            for k in range(4, Y):
+                first_piece(k, order[k])
+                if k < Y - 1:
+                    send_columns(0, k)
+            load_x.wait()
+            load_w.wait()
+            part = jnp.dot(xall[y], wv[...], preferred_element_type=F32)
+            bpart[...] = part.reshape(N, OWN, BOT)
             for d in FAR8:
                 send(bpart.at[lax.rem(n + d, N)], brecv.at[d - 1], PH_B, recv_sem.at[PH_B], dev_n(d))
         else:
@@ -254,13 +269,15 @@
                     acc = acc + tv
                     gbuf[:, s * LANES : (s + 1) * LANES] = (tv * inv_col[p, s : s + 1, :]).astype(BF16)
                 part = lax.dot_general(gbuf[...], raw[p], NT, preferred_element_type=F32)
-                part = part.reshape(N, OWN, BOT)
                 if k == 0:
-                    tgm[:, :, :BOT] = part
+                    tgf[...] = part
                 else:
-                    tgm[:, :, :BOT] += part
+                    tgf[...] += part
         if it < ITERS - 1:
-            nsrc[it] = jnp.sum(acc.T, 0, keepdims=True)
+            tile = row_tile(acc, 0)
+            if it == TOTALS:
+                tile = tile + row_tile(egm[:, :, BOT:].reshape(ROWS, LANES), GROUPS)
+            nsrc[it] = tile
             for d in FAR8:
                 send(nsrc.at[it], nrecv.at[it, d - 1], ph + 3, recv_sem.at[ph + 3], dev_n(d))
             beside(it, "n")
@@ -269,19 +286,34 @@
             for d in range(N - 1):
                 total = total + nrecv[it, d]
             scale = 1.0 / (CROPS * total)
-            ub[...] = jnp.broadcast_to(scale, (LANES, ROWS)).T
+            for g in range(GROUPS):
+                ub[8 * g : 8 * g + 8, :] = jnp.broadcast_to(scale[:, g : g + 1], (8, LANES))
+            if it == TOTALS:
+                for g in range(GROUPS):
+                    ratio = scale[:, GROUPS + g : GROUPS + g + 1] / scale[:, g : g + 1]
+                    kappa[8 * g : 8 * g + 8, :] = jnp.broadcast_to(ratio, (8, LANES))
         else:
-            tgm[:, :, BOT:] = acc.reshape(N, OWN, LANES)
+            kap = kappa[...]
+            for j in range(BOT // LANES):
+                at = slice(j * LANES, (j + 1) * LANES)
+                less = tgf[:, at] - kap * egm[:, :, at].reshape(ROWS, LANES)
+                tgm[:, :, at] = less.astype(BF16).reshape(N, OWN, LANES)
+            high = acc.astype(BF16)
+            tgm[:, :, BOT : BOT + LANES] = high.reshape(N, OWN, LANES)
+            low = (acc - high.astype(F32)).astype(BF16)
+            tgm[:, :, BOT + LANES :] = low.reshape(N, OWN, LANES)
 
     for d in FAR8:
         send(tgm.at[lax.rem(n + d, N)], tgr.at[d - 1], PH_TG, recv_sem.at[PH_TG], dev_n(d))
     wait_all(tgr, recv_sem.at[PH_TG])
-    t = tgm[n]
+    t = tgm[n].astype(F32)
     for d in range(N - 1):
-        t = t + tgr[d]
-    scale = 1.0 / (CROPS * jnp.sum(t[:, BOT:], 1, keepdims=True))
+        t = t + tgr[d].astype(F32)
+    row_mass = jnp.sum(t[:, BOT : BOT + LANES] + t[:, BOT + LANES :], 1, keepdims=True)
+    scale = 1.0 / (CROPS * row_mass)
     unit = unit_own[...]
-    ug = (eg_own[...] - t[:, :BOT] * (scale * CROPS)) * (1.0 / STUDENT_TEMP)
+    teacher = t[:, :BOT] + eg_less[...]
+    ug = (eg_own[...] - teacher * (scale * CROPS)) * (1.0 / STUDENT_TEMP)
     radial = jnp.sum(unit * ug, 1, keepdims=True)
     bgall[n] = (inv_own[:, :1] * (ug - unit * radial)).astype(BF16)
     for d in FAR8:
@@ -327,7 +359,8 @@
     out = gwz[z]
     for d in range(Z - 1):
         out = out + gwr[d]
-    gw_ref[...] = out
+    gw_ref[:, :LANES] = out[:4]
+    gw_ref[:, LANES:] = out[4:]
 
 
 def shards(crop_hidden, bottleneck_weight, prototypes, teacher_scores):
@@ -336,10 +369,10 @@
     gh, gw = pl.pallas_call(
         kernel,
         out_shape=(
-            jax.ShapeDtypeStruct((ROWS, HIDB), BF16),
-            jax.ShapeDtypeStruct((8, LANES), F32),
+            pltpu.VMEM((ROWS, HIDB), BF16),
+            pltpu.VMEM((4, HIDB), F32),
         ),
-        in_specs=[pl.BlockSpec(memory_space=pl.ANY)] * 4,
+        in_specs=[pl.BlockSpec(memory_space=pltpu.HBM)] * 4,
         out_specs=(pl.BlockSpec(memory_space=vmem), pl.BlockSpec(memory_space=vmem)),
         scratch_shapes=[
             vmem((Y, ROWS, PIECE), BF16),
@@ -353,8 +386,9 @@
             vmem((ITERS, SUB, LANES), F32),
             vmem((ITERS, Z - 1, SUB, LANES), F32),
             vmem((ITERS, Y, SUB, LANES), F32),
-            vmem((ITERS - 1, 1, ROWS), F32),
-            vmem((ITERS - 1, N - 1, 1, ROWS), F32),
+            vmem((ITERS - 1, 8, LANES), F32),
+            vmem((ITERS - 1, N - 1, 8, LANES), F32),
+            vmem((ROWS, LANES), F32),
             vmem((ROWS, LANES), F32),
             vmem((N, OWN, BOT), F32),
             vmem((N - 1, OWN, BOT), F32),
@@ -366,8 +400,10 @@
             vmem((N, OWN, WIDE), F32),
             vmem((N - 1, OWN, WIDE), F32),
             vmem((OWN, BOT), F32),
-            vmem((N, OWN, WIDE), F32),
-            vmem((N - 1, OWN, WIDE), F32),
+            vmem((OWN, BOT), F32),
+            vmem((ROWS, BOT), F32),
+            vmem((N, OWN, WIDE + LANES), BF16),
+            vmem((N - 1, OWN, WIDE + LANES), BF16),
             vmem((N, OWN, BOT), BF16),
             vmem((BOT, BOT), BF16),
             vmem((Y, GROUP, ROWS), BF16),
@@ -383,12 +419,11 @@
             pltpu.SemaphoreType.DMA((Y - 1,)),
         ],
         compiler_params=pltpu.CompilerParams(
-            collective_id=0, has_side_effects=True, vmem_limit_bytes=60 * 1024 * 1024
+            collective_id=0, has_side_effects=True, vmem_limit_bytes=58 * 1024 * 1024
         ),
         name="sinkhorn_head",
     )(crop_hidden, bottleneck_weight, prototypes, teacher_scores)
-    half = HIDB // 2
-    return gh, jnp.concatenate([gw[:4, :half], gw[4:, :half]], axis=1)
+    return gh, gw
 
 
 def solution(mesh):

time: 95.2 us -> 92.5 us (0.972)
  local copies, waits for them, and re-layouts: 2.24 us -> 1.22 us
  Pallas kernels: 91.5 us -> 90.5 us
    pallas_call x1, Pallas kernels: 91.5 us -> 90.5 us  [shards(): pl.pallas_call(kernel, out_shape=(pltpu.VMEM((ROWS, HIDB), BF16), pltpu.V...]
where the time goes in v2:
time: 92.5 us; the launch traced here: 92.4 us
  Pallas kernels  90.5 us (98%)
  local copies, waits for them, and re-layouts  1.22 us (1%)
    pallas_call x1, Pallas kernels, shards(): pl.pallas_call(kernel, out_shape=(pltpu.VMEM((ROWS, HIDB), BF16), pltpu.V...  90.5 us

profile of v2, /device:TPU:1, one launch (start us, length us, event | category | flops | bytes accessed | tf_op | source)
XLA Modules:
  0.0 92.4 jit_solution(4885723093761840084)
XLA Ops:
  0.6 90.5 %sinkhorn_head.1 = (bf16[128,256]{1,0:T(8,128)(2,1)S(1)}, f32[4,256]{1,0:T(4,128)S(1)}) custom-call(bf16[128,256]{1,0:T(8,128)(2,1)} %x_hbm.1, bf16[256,384]{1,0:T(8,128)(2,1)} %w_hbm.1, bf16[384,8192]{1,0:T(8,128)(2,1)} %p_hbm.1, bf16[128,8192]{1,0:T(8,128)(2,1)} %t_hbm.1), custom_call_target="tpu_custom_call" | custom-call | tf_op jit(solution)/shard_map/sinkhorn_head/pallas_call | solution.py:369
  91.2 0.6 copy.8
  91.8 0.6 copy.9

commit v3 on v2

--- a/solution.py
+++ b/solution.py
@@ -19,6 +19,8 @@
 LANES = 128
 PIECE = COLS // Y
 SUB = PIECE // LANES
+HALF = Y // 2
+BSUB = 2 * SUB
 HIDB = 2048 // N
 WIDE = BOT + LANES
 GROUPS = ROWS // 8
@@ -31,13 +33,15 @@
 
 FAR8 = (4, 3, 5, 2, 6, 1, 7)
 NEAR8 = (1, 7, 2, 6, 3, 5, 4)
+BLOCKS = (0, 3, 1, 2)
+NEXT = (1, 7, 2)
 FAR12 = (6, 5, 7, 4, 8, 3, 9, 2, 10, 1, 11)
 NT = (((1,), (1,)), ((), ()))
 
 
 def kernel(
     x_hbm, w_hbm, p_hbm, t_hbm, gh_ref, gw_ref,
-    tin, raw, wv, xall, texp, inv_col, cbuf, yrecv, zsrc, zrecv, vall,
+    tin, raw, wv, xall, texp, inv_col, cf, cbuf, yrecv, zsrc, zrecv, vall,
     nsrc, nrecv, ub, kappa, bpart, brecv, ball, unit_own, inv_own, sbuf, gbuf,
     egm, egr, eg_own, eg_less, tgf, tgm, tgr, bgall, perm, bts, btr, gwf, gwz, gwr,
     load_sem, proto_sem, send_sem, recv_sem, v_sem, bt_sem,
@@ -64,7 +68,8 @@
     for d in FAR8:
         pl.semaphore_signal(barrier, inc=1, device_id=dev_n(d), device_id_type=MESH)
 
-    order = [lax.rem(y + d, Y) for d in FAR8] + [y]
+    blocks = [lax.rem(y + d, HALF) for d in BLOCKS]
+    order = [2 * q + h for q in blocks for h in range(2)]
     load_x = pltpu.make_async_copy(x_hbm, xall.at[y], load_sem.at[0])
     load_w = pltpu.make_async_copy(w_hbm, wv, load_sem.at[1])
 
@@ -98,23 +103,32 @@
 
     PH_B, PH_U, PH_X, PH_EG, PH_TG, PH_BG, PH_BT, PH_GW, PH_IT = range(9)
 
-    def first_piece(k, p):
-        load_t[k].wait()
-        for s in range(SUB):
-            e = jnp.exp(tin[p, :, s * LANES : (s + 1) * LANES].astype(F32) * (1.0 / TEACHER_TEMP))
-            texp[p * SUB + s] = e
-            cbuf[0, p, s : s + 1, :] = jnp.sum(e, 0, keepdims=True)
-
-    def mass_piece(it, p, rows):
-        for s in range(SUB):
-            cbuf[it, p, s : s + 1, :] = jnp.sum(texp[p * SUB + s] * rows, 0, keepdims=True)
+    def first_block(k):
+        for h in range(2):
+            p = order[2 * k + h]
+            load_t[2 * k + h].wait()
+            for s in range(SUB):
+                e = jnp.exp(
+                    tin[p, :, s * LANES : (s + 1) * LANES].astype(F32) * (1.0 / TEACHER_TEMP)
+                )
+                texp[p * SUB + s] = e
+                row = h * SUB + s
+                cf[k, row : row + 1, :] = jnp.sum(e, 0, keepdims=True)
+        cbuf[0, blocks[k]] = cf[k].astype(BF16)
+
+    def mass_block(it, k, rows):
+        for s in range(BSUB):
+            cf[k, s : s + 1, :] = jnp.sum(texp[blocks[k] * BSUB + s] * rows, 0, keepdims=True)
+        cbuf[it, blocks[k]] = cf[k].astype(BF16)
 
     def send_columns(it, k):
-        d = FAR8[k]
-        send(
-            cbuf.at[it, order[k]], yrecv.at[it, d - 1],
-            PH_IT + 4 * it, recv_sem.at[PH_IT + 4 * it], dev_y(d),
-        )
+        far = (BLOCKS[k] + HALF) % Y
+        for d in (far, BLOCKS[k]) if far in (4, 5) else (BLOCKS[k], far):
+            if d:
+                send(
+                    cbuf.at[it, blocks[k]], yrecv.at[it, d - 1],
+                    PH_IT + 4 * it, recv_sem.at[PH_IT + 4 * it], dev_y(d),
+                )
 
     def norm_piece(p):
         load_p[p].wait()
@@ -217,15 +231,14 @@
     for it in range(ITERS):
         ph = PH_IT + 4 * it
         if it == 0:
-            for k in range(4):
-                first_piece(k, order[k])
+            for k in range(2):
+                first_block(k)
             pl.semaphore_wait(barrier, (Z - 1) + (Y - 1) + (N - 1))
-            for k in range(4):
+            for k in range(2):
                 send_columns(0, k)
-            for k in range(4, Y):
-                first_piece(k, order[k])
-                if k < Y - 1:
-                    send_columns(0, k)
+            for k in range(2, HALF):
+                first_block(k)
+                send_columns(0, k)
             load_x.wait()
             load_w.wait()
             part = jnp.dot(xall[y], wv[...], preferred_element_type=F32)
@@ -234,42 +247,45 @@
                 send(bpart.at[lax.rem(n + d, N)], brecv.at[d - 1], PH_B, recv_sem.at[PH_B], dev_n(d))
         else:
             rows = ub[...]
-            for k in range(Y):
-                mass_piece(it, order[k], rows)
-                if k < Y - 1:
-                    send_columns(it, k)
+            for k in range(HALF):
+                mass_block(it, k, rows)
+                send_columns(it, k)
         beside(it, "y")
         wait_all(yrecv.at[it], recv_sem.at[ph])
-        mass = cbuf[it, y]
+        mine = blocks[0]
+        mass = cbuf[it, mine].astype(F32)
         for d in range(Y - 1):
-            mass = mass + yrecv[it, d]
-        zsrc[it] = mass
+            mass = mass + yrecv[it, d].astype(F32)
+        zsrc[it] = mass.astype(BF16)
         for d in FAR12:
             send(zsrc.at[it], zrecv.at[it, d - 1], ph + 1, recv_sem.at[ph + 1], dev_z(d))
         beside(it, "z")
         wait_all(zrecv.at[it], recv_sem.at[ph + 1])
         for d in range(Z - 1):
-            mass = mass + zrecv[it, d]
-        vall[it, y] = 1.0 / (PROTO * mass)
-        for d in FAR8:
-            send(vall.at[it, y], vall.at[it, y], ph + 2, v_sem.at[it, d - 1], dev_y(d))
+            mass = mass + zrecv[it, d].astype(F32)
+        vall[it, mine] = 1.0 / (PROTO * mass)
+        for j in (2, 0, 1):
+            send(vall.at[it, mine], vall.at[it, mine], ph + 2, v_sem.at[it, j], dev_y(NEXT[j]))
         beside(it, "v")
 
         acc = jnp.zeros((ROWS, LANES), F32)
-        for k, d in enumerate((0,) + NEAR8):
-            p = lax.rem(y - d + Y, Y)
-            if d:
-                wait_all(vall.at[it, p], v_sem.at[it, d - 1])
+        for k, d in enumerate((0,) + NEXT):
+            q = lax.rem(y - d + Y, HALF)
+            if k:
+                wait_all(vall.at[it, q], v_sem.at[it, k - 1])
             if it < ITERS - 1:
+                for s in range(BSUB):
+                    acc = acc + texp[q * BSUB + s] * vall[it, q, s : s + 1, :]
+                continue
+            for h in range(2):
+                p = 2 * q + h
                 for s in range(SUB):
-                    acc = acc + texp[p * SUB + s] * vall[it, p, s : s + 1, :]
-            else:
-                for s in range(SUB):
-                    tv = texp[p * SUB + s] * vall[it, p, s : s + 1, :]
+                    row = h * SUB + s
+                    tv = texp[p * SUB + s] * vall[it, q, row : row + 1, :]
                     acc = acc + tv
                     gbuf[:, s * LANES : (s + 1) * LANES] = (tv * inv_col[p, s : s + 1, :]).astype(BF16)
                 part = lax.dot_general(gbuf[...], raw[p], NT, preferred_element_type=F32)
-                if k == 0:
+                if k == 0 and h == 0:
                     tgf[...] = part
                 else:
                     tgf[...] += part
@@ -351,7 +367,7 @@
         ph = PH_IT + 4 * it
         wait_all(yrecv.at[it], send_sem.at[ph])
         wait_all(zrecv.at[it], send_sem.at[ph + 1])
-        wait_all(vall.at[it, pl.ds(0, Y - 1)], send_sem.at[ph + 2])
+        wait_all(vall.at[it, pl.ds(0, len(NEXT))], send_sem.at[ph + 2])
         if it < ITERS - 1:
             wait_all(nrecv.at[it], send_sem.at[ph + 3])
     wait_all(gwr, send_sem.at[PH_GW])
@@ -381,11 +397,12 @@
             vmem((Y, ROWS, HIDB), BF16),
             vmem((Y * SUB, ROWS, LANES), F32),
             vmem((Y, SUB, LANES), F32),
-            vmem((ITERS, Y, SUB, LANES), F32),
-            vmem((ITERS, Y - 1, SUB, LANES), F32),
-            vmem((ITERS, SUB, LANES), F32),
-            vmem((ITERS, Z - 1, SUB, LANES), F32),
-            vmem((ITERS, Y, SUB, LANES), F32),
+            vmem((HALF, BSUB, LANES), F32),
+            vmem((ITERS, HALF, BSUB, LANES), BF16),
+            vmem((ITERS, Y - 1, BSUB, LANES), BF16),
+            vmem((ITERS, BSUB, LANES), BF16),
+            vmem((ITERS, Z - 1, BSUB, LANES), BF16),
+            vmem((ITERS, HALF, BSUB, LANES), F32),
             vmem((ITERS - 1, 8, LANES), F32),
             vmem((ITERS - 1, N - 1, 8, LANES), F32),
             vmem((ROWS, LANES), F32),
@@ -415,7 +432,7 @@
             pltpu.SemaphoreType.DMA((Y,)),
             pltpu.SemaphoreType.DMA((phases,)),
             pltpu.SemaphoreType.DMA((phases,)),
-            pltpu.SemaphoreType.DMA((ITERS, Y - 1)),
+            pltpu.SemaphoreType.DMA((ITERS, len(NEXT))),
             pltpu.SemaphoreType.DMA((Y - 1,)),
         ],
         compiler_params=pltpu.CompilerParams(

time: 92.5 us -> 90.2 us (0.975)
  Pallas kernels: 90.5 us -> 87.6 us
    pallas_call x1, Pallas kernels: 90.5 us -> 87.6 us  [shards(): pl.pallas_call(kernel, out_shape=(pltpu.VMEM((ROWS, HIDB), BF16), pltpu.V...]
where the time goes in v3:
time: 90.2 us; the launch traced here: 89.5 us
  Pallas kernels  87.6 us (97%)
  local copies, waits for them, and re-layouts  1.22 us (1%)
    pallas_call x1, Pallas kernels, shards(): pl.pallas_call(kernel, out_shape=(pltpu.VMEM((ROWS, HIDB), BF16), pltpu.V...  87.6 us

profile of v3, /device:TPU:1, one launch (start us, length us, event | category | flops | bytes accessed | tf_op | source)
XLA Modules:
  0.0 89.5 jit_solution(2162362160279784959)
XLA Ops:
  0.6 87.6 %sinkhorn_head.1 = (bf16[128,256]{1,0:T(8,128)(2,1)S(1)}, f32[4,256]{1,0:T(4,128)S(1)}) custom-call(bf16[128,256]{1,0:T(8,128)(2,1)} %x_hbm.1, bf16[256,384]{1,0:T(8,128)(2,1)} %w_hbm.1, bf16[384,8192]{1,0:T(8,128)(2,1)} %p_hbm.1, bf16[128,8192]{1,0:T(8,128)(2,1)} %t_hbm.1), custom_call_target="tpu_custom_call" | custom-call | tf_op jit(solution)/shard_map/sinkhorn_head/pallas_call | solution.py:385
  88.2 0.6 copy.8
  88.9 0.6 copy.9

commit v4 on v3

--- a/solution.py
+++ b/solution.py
@@ -263,7 +263,7 @@
         wait_all(zrecv.at[it], recv_sem.at[ph + 1])
         for d in range(Z - 1):
             mass = mass + zrecv[it, d].astype(F32)
-        vall[it, mine] = 1.0 / (PROTO * mass)
+        vall[it, mine] = (1.0 / (PROTO * mass)).astype(BF16)
         for j in (2, 0, 1):
             send(vall.at[it, mine], vall.at[it, mine], ph + 2, v_sem.at[it, j], dev_y(NEXT[j]))
         beside(it, "v")
@@ -273,15 +273,16 @@
             q = lax.rem(y - d + Y, HALF)
             if k:
                 wait_all(vall.at[it, q], v_sem.at[it, k - 1])
+            v = vall[it, q].astype(F32)
             if it < ITERS - 1:
                 for s in range(BSUB):
-                    acc = acc + texp[q * BSUB + s] * vall[it, q, s : s + 1, :]
+                    acc = acc + texp[q * BSUB + s] * v[s : s + 1]
                 continue
             for h in range(2):
                 p = 2 * q + h
                 for s in range(SUB):
                     row = h * SUB + s
-                    tv = texp[p * SUB + s] * vall[it, q, row : row + 1, :]
+                    tv = texp[p * SUB + s] * v[row : row + 1]
                     acc = acc + tv
                     gbuf[:, s * LANES : (s + 1) * LANES] = (tv * inv_col[p, s : s + 1, :]).astype(BF16)
                 part = lax.dot_general(gbuf[...], raw[p], NT, preferred_element_type=F32)
@@ -402,7 +403,7 @@
             vmem((ITERS, Y - 1, BSUB, LANES), BF16),
             vmem((ITERS, BSUB, LANES), BF16),
             vmem((ITERS, Z - 1, BSUB, LANES), BF16),
-            vmem((ITERS, HALF, BSUB, LANES), F32),
+            vmem((ITERS, HALF, BSUB, LANES), BF16),
             vmem((ITERS - 1, 8, LANES), F32),
             vmem((ITERS - 1, N - 1, 8, LANES), F32),
             vmem((ROWS, LANES), F32),

time: 90.2 us -> 89.5 us (level)
  no operation moved by 1% of the time
where the time goes in v4:
time: 89.5 us; the launch traced here: 89.2 us
  Pallas kernels  87.4 us (98%)
  local copies, waits for them, and re-layouts  1.22 us (1%)
    pallas_call x1, Pallas kernels, shards(): pl.pallas_call(kernel, out_shape=(pltpu.VMEM((ROWS, HIDB), BF16), pltpu.V...  87.4 us

profile of v4, /device:TPU:1, one launch (start us, length us, event | category | flops | bytes accessed | tf_op | source)
XLA Modules:
  0.0 89.2 jit_solution(8894735731155037189)
XLA Ops:
  0.6 87.4 %sinkhorn_head.1 = (bf16[128,256]{1,0:T(8,128)(2,1)S(1)}, f32[4,256]{1,0:T(4,128)S(1)}) custom-call(bf16[128,256]{1,0:T(8,128)(2,1)} %x_hbm.1, bf16[256,384]{1,0:T(8,128)(2,1)} %w_hbm.1, bf16[384,8192]{1,0:T(8,128)(2,1)} %p_hbm.1, bf16[128,8192]{1,0:T(8,128)(2,1)} %t_hbm.1), custom_call_target="tpu_custom_call" | custom-call | tf_op jit(solution)/shard_map/sinkhorn_head/pallas_call | solution.py:386
  88.0 0.6 copy.8
  88.6 0.6 copy.9
